TPU v7x, 32 devices: a whole 2x2x4 slice. The times are simulated.
32 devices in a mesh: dp: 4 (over x, core), adapter: 8 (over z, y).
Axes of the slice: x: 2, y: 2, z: 4, core: 2. Of those that a mesh axis runs over, the one named last changes fastest.
Arguments:
- tokens: bfloat16 [4096, 8192], P(('dp', 'adapter')), may hold values from -6 to 6
- grad_out: bfloat16 [4096, 8192], P(('dp', 'adapter')), may hold values from -6 to 6
- down_panels: bfloat16 [16, 8192, 64], P('adapter'), may hold values from -0.0625 to 0.0625
- up_panels: bfloat16 [16, 64, 8192], P('adapter'), may hold values from -0.75 to 0.75
- seg_adapter: int32 [64], P(('dp', 'adapter')), may hold values from 0 to 15, as said below
Outputs:
- adapter_out: bfloat16 [4096, 8192], P(('dp', 'adapter'))
- grad_tokens: bfloat16 [4096, 8192], P(('dp', 'adapter'))
- grad_down: bfloat16 [16, 8192, 64], P('adapter', 'dp')
- grad_up: bfloat16 [16, 64, 8192], P('adapter', None, 'dp')
Inputs may be any that keep to these rules, and one draw needn't show every extreme that they name: `seg_adapter`: adapter a is held by index a // 2 of the adapter axis. A segment of the device at index j of the adapter axis names a holder (j + k) modulo the axis's size, with k from 0 to 3; the 2 segments of one device name different holders, and in every data group some holder is named by 4 segments.
All inputs are finite; a program needn't handle non-finite values.
Results may differ from a plain program's by a relative error of at most 0.0049.
Values may be sent and summed in bfloat16 or wider, within the bound.
A program may use at most 128 MiB of HBM per device.

v0:
```python
import jax
import jax.numpy as jnp
from jax import lax
from jax.sharding import PartitionSpec as P

adapter_scale = 2.0


def shifted(value, axis, steps):
    count = lax.axis_size(axis)
    pairs = [(source, (source + steps) % count) for source in range(count)]
    return lax.ppermute(value, axis, pairs)


def slot_mask(selector, held_count, rank_size):
    picks = (
        selector.astype(jnp.float32) == jnp.arange(held_count, dtype=jnp.float32)[None, :]
    ).astype(jnp.float32)
    return jnp.repeat(picks, rank_size, axis=1)[:, None, :]


def on_device(tokens, grad_out, down_panels, up_panels, seg_adapter):
    groups = lax.axis_size("adapter")
    held_count, feat_width, rank_size = down_panels.shape
    segs_here = seg_adapter.shape[0]
    seg_rows = tokens.shape[0] // segs_here
    reach_count = 2 * segs_here
    position = lax.axis_index("adapter")
    owners_of = seg_adapter // held_count
    local_index = seg_adapter - owners_of * held_count
    distance = jnp.mod(owners_of - position, groups)
    placing = jnp.arange(reach_count, dtype=jnp.int32)[:, None] == distance[None, :]
    place_bf = placing.astype(jnp.bfloat16)
    selector = (jnp.sum(jnp.where(placing, local_index[None, :] + 1, 0), axis=1) - 1).astype(
        jnp.bfloat16
    )[:, None]
    down_cat = jnp.transpose(down_panels, (1, 0, 2)).reshape(feat_width, held_count * rank_size)
    up_weight_joined = up_panels.reshape(held_count * rank_size, feat_width)

    def pack_rows(token_rows):
        blocks = token_rows.reshape(segs_here, seg_rows, feat_width)
        return jnp.einsum(
            "ns,sjd->njd", place_bf, blocks, preferred_element_type=jnp.float32
        ).astype(jnp.bfloat16)

    def unpack(slot_rows):
        placed = jnp.einsum("ns,njd->sjd", place_bf, slot_rows, preferred_element_type=jnp.float32)
        return placed.astype(jnp.bfloat16).reshape(tokens.shape)

    sent_rows = pack_rows(tokens)
    sent_grads = pack_rows(grad_out)
    rows_list = [sent_rows[slot_index] for slot_index in range(reach_count)]
    grads_list = [sent_grads[slot_index] for slot_index in range(reach_count)]
    select_list = [selector[slot_index] for slot_index in range(reach_count)]
    for slot_index in range(1, reach_count):
        moved = shifted(
            (rows_list[slot_index], grads_list[slot_index], select_list[slot_index]),
            "adapter",
            slot_index,
        )
        rows_list[slot_index], grads_list[slot_index], select_list[slot_index] = moved
    arrived_rows = jnp.stack(rows_list)
    arrived_grads = jnp.stack(grads_list)
    arrived_select = jnp.stack(select_list)
    masking = slot_mask(arrived_select, held_count, rank_size)
    hidden_state = (
        jnp.einsum("njd,dc->njc", arrived_rows, down_cat, preferred_element_type=jnp.float32)
        * masking
    ).astype(jnp.bfloat16)
    projected_output = (
        adapter_scale
        * jnp.einsum(
            "qfs,su->qfu", hidden_state, up_weight_joined, preferred_element_type=jnp.float32
        )
    ).astype(jnp.bfloat16)
    hidden_gradient = adapter_scale * jnp.einsum(
        "njd,cd->njc", arrived_grads, up_weight_joined, preferred_element_type=jnp.float32
    )
    hidden_gradient = (hidden_gradient * masking).astype(jnp.bfloat16)
    grad_rows = jnp.einsum(
        "njc,dc->njd", hidden_gradient, down_cat, preferred_element_type=jnp.float32
    ).astype(jnp.bfloat16)
    down_sum = jnp.einsum(
        "njd,njc->dc", arrived_rows, hidden_gradient, preferred_element_type=jnp.float32
    )
    down_sum = jnp.transpose(down_sum.reshape(feat_width, held_count, rank_size), (1, 0, 2))
    up_weight_sum = adapter_scale * jnp.einsum(
        "njc,njd->cd", hidden_state, arrived_grads, preferred_element_type=jnp.float32
    )
    up_weight_sum = up_weight_sum.reshape(held_count, rank_size, feat_width)
    result_list = [projected_output[slot_index] for slot_index in range(reach_count)]
    back_list = [grad_rows[slot_index] for slot_index in range(reach_count)]
    for slot_index in range(1, reach_count):
        moved = shifted((result_list[slot_index], back_list[slot_index]), "adapter", -slot_index)
        result_list[slot_index], back_list[slot_index] = moved
    adapter_out = unpack(jnp.stack(result_list))
    grad_tokens = unpack(jnp.stack(back_list))
    grad_down, grad_up = (
        lax.psum_scatter(down_sum, "dp", scatter_dimension=1, tiled=True),
        lax.psum_scatter(up_weight_sum, "dp", scatter_dimension=2, tiled=True),
    )
    return (adapter_out, grad_tokens, grad_down.astype(jnp.bfloat16), grad_up.astype(jnp.bfloat16))


def solution(mesh):
    placed = (
        P(("dp", "adapter"), None),
        P(("dp", "adapter"), None),
        P("adapter", None, None),
        P("adapter", None, None),
        P(("dp", "adapter")),
    )
    return jax.shard_map(
        on_device,
        mesh=mesh,
        in_specs=placed,
        out_specs=(
            P(("dp", "adapter"), None),
            P(("dp", "adapter"), None),
            P("adapter", "dp", None),
            P("adapter", None, "dp"),
        ),
        check_vma=False,
    )
```

profile of v0, /device:TPU:29, one launch (start us, length us, event | category | flops | bytes accessed | tf_op | source)
XLA Modules:
  0.0 455.4 jit_solution(7417159244240837635)
XLA Ops:
  12.2 5.8 %convolution_convert_fusion.2 = bf16[4,64,8192]{2,0,1:T(4,128)(2,1)S(1)} fusion(bf16[2,64,8192]{2,1,0:T(8,128)(2,1)} %bitcast.99, s32[2]{0:T(128)S(1)} %and_select_fusion), kind=kOutput, calls=%fused_computation.4 | convolution fusion | flops 10485768 | bytes 6291464 | tf_op jit(solution)/shard_map/ns,sjd->njd/dot_general | solution.py:42
  18.1 10.0 %fusion.38 = (bf16[1,64,8192]{2,0,1:T(2,128)(2,1)}, bf16[1,64,8192]{2,0,1:T(2,128)(2,1)S(1)}, bf16[1,64,8192]{2,0,1:T(2,128)(2,1)S(1)}, bf16[1,64,8192]{2,0,1:T(2,128)(2,1)S(1)}) fusion(bf16[4,64,8192]{2,0,1:T(4,128)(2,1)S(1)} %convolution_convert_fusion.2), kind=kLoop, calls=%fused_computation.67 | loop fusion | bytes 8388608 | tf_op jit(solution)/shard_map/slice | solution.py:52
  32.9 3.8 convolution_convert_fusion.1
  36.7 10.0 %fusion.36 = (bf16[1,64,8192]{2,0,1:T(2,128)(2,1)}, bf16[1,64,8192]{2,0,1:T(2,128)(2,1)S(1)}, bf16[1,64,8192]{2,0,1:T(2,128)(2,1)S(1)}, bf16[1,64,8192]{2,0,1:T(2,128)(2,1)S(1)}) fusion(bf16[4,64,8192]{2,0,1:T(4,128)(2,1)S(1)} %convolution_convert_fusion.1), kind=kLoop, calls=%fused_computation.65 | loop fusion | bytes 8388608 | tf_op jit(solution)/shard_map/slice | solution.py:53
  59.9 2.5 maximum_convert_fusion
  62.7 3.5 copy.56
  66.2 9.5 %collective-permute-done.1 = bf16[64,8192]{1,0:T(8,128)(2,1)} collective-permute-done((bf16[64,8192]{1,0:T(8,128)(2,1)}, bf16[64,8192]{1,0:T(8,128)(2,1)}, u32[]{:S(2)}, u32[]{:S(2)}) %collective-permute-start.1) | collective-permute-done | bytes 1048608 | tf_op jit(solution)/shard_map/ppermute | solution.py:12
  75.7 3.5 copy.57
  79.2 17.3 %collective-permute-done.2 = bf16[64,8192]{1,0:T(8,128)(2,1)} collective-permute-done((bf16[64,8192]{1,0:T(8,128)(2,1)}, bf16[64,8192]{1,0:T(8,128)(2,1)}, u32[]{:S(2)}, u32[]{:S(2)}) %collective-permute-start.2) | collective-permute-done | bytes 1048608 | tf_op jit(solution)/shard_map/ppermute | solution.py:12
  96.5 3.5 copy.58
  100.1 19.3 %collective-permute-done.9 = bf16[64,8192]{1,0:T(8,128)(2,1)} collective-permute-done((bf16[64,8192]{1,0:T(8,128)(2,1)}, bf16[64,8192]{1,0:T(8,128)(2,1)}, u32[]{:S(2)}, u32[]{:S(2)}) %collective-permute-start.9) | collective-permute-done | bytes 1048608 | tf_op jit(solution)/shard_map/ppermute | solution.py:12
  119.4 3.7 copy.64
  123.1 19.3 %collective-permute-done.10 = bf16[64,8192]{1,0:T(8,128)(2,1)} collective-permute-done((bf16[64,8192]{1,0:T(8,128)(2,1)}, bf16[64,8192]{1,0:T(8,128)(2,1)}, u32[]{:S(2)}, u32[]{:S(2)}) %collective-permute-start.10) | collective-permute-done | bytes 1048608 | tf_op jit(solution)/shard_map/ppermute | solution.py:12
  142.4 3.5 copy.65
  145.9 18.3 %collective-permute-done.11 = bf16[64,8192]{1,0:T(8,128)(2,1)} collective-permute-done((bf16[64,8192]{1,0:T(8,128)(2,1)S(1)}, bf16[64,8192]{1,0:T(8,128)(2,1)}, u32[]{:S(2)}, u32[]{:S(2)}) %collective-permute-start.11) | collective-permute-done | bytes 1048608 | tf_op jit(solution)/shard_map/ppermute | solution.py:12
  164.2 3.5 copy.66
  167.8 20.5 %pad_maximum_fusion.2 = bf16[4,64,8192]{2,0,1:T(4,128)(2,1)S(1)} fusion(bf16[1,64,8192]{2,0,1:T(2,128)(2,1)S(1)} %copy.66, bf16[1,64,8192]{2,0,1:T(2,128)(2,1)S(1)} %copy.65, bf16[1,64,8192]{2,0,1:T(2,128)(2,1)S(1)} %copy.64, bf16[1,64,8192]{2,0,1:T(2,128)(2,1)S(1)} %copy-done.5), kind=kLoop, calls=%fused_computation.11 | loop fusion | flops 16777216 | bytes 8388608 | tf_op jit(solution)/shard_map/stack | solution.py:63
  188.3 4.8 %fusion.19 = bf16[4,64,128]{2,1,0:T(8,128)(2,1)S(1)} fusion(bf16[128,8192,1]{1,0,2:T(8,128)(2,1)S(1)} %bitcast.83, bf16[4,64,8192]{2,0,1:T(4,128)(2,1)S(1)} %pad_maximum_fusion.2, f32[4,128]{1,0:T(4,128)S(1)} %broadcast_multiply_fusion), kind=kOutput, calls=%fused_computation.26 | convolution fusion | flops 536936448 | bytes 6359040 | tf_op jit(solution)/shard_map/njd,cd->njc/dot_general | solution.py:76
  193.2 9.8 %pad_maximum_fusion = bf16[4,64,8192]{2,0,1:T(4,128)(2,1)S(1)} fusion(bf16[1,64,8192]{2,0,1:T(2,128)(2,1)S(1)} %copy.58, bf16[1,64,8192]{2,0,1:T(2,128)(2,1)S(1)} %copy.57, bf16[1,64,8192]{2,0,1:T(2,128)(2,1)S(1)} %copy.56, bf16[1,64,8192]{2,0,1:T(2,128)(2,1)S(1)} %copy-done.4), kind=kLoop, calls=%fused_computation.9 | loop fusion | flops 16777216 | bytes 8388608 | tf_op jit(solution)/shard_map/stack | solution.py:62
  203.0 6.9 %fusion.7 = f32[8192,128,1]{0,1,2:T(8,128)} fusion(bf16[4,64,128]{2,1,0:T(8,128)(2,1)S(1)} %fusion.19, bf16[4,64,8192]{2,0,1:T(4,128)(2,1)S(1)} %pad_maximum_fusion), kind=kOutput, calls=%fused_computation.18 | convolution fusion | flops 536870912 | bytes 8454144 | tf_op jit(solution)/shard_map/njd,njc->dc/dot_general | solution.py:83
  210.2 7.7 %fusion.22 = bf16[4,64,128]{2,1,0:T(8,128)(2,1)S(1)} fusion(bf16[8192,128,1]{0,1,2:T(8,128)(2,1)} %bitcast.88, bf16[4,64,8192]{2,0,1:T(4,128)(2,1)} %copy-done.1, f32[4,128]{1,0:T(4,128)S(1)} %mul.40), kind=kOutput, calls=%fused_computation.27 | convolution fusion | flops 536936448 | bytes 6359040 | tf_op jit(solution)/shard_map/njd,dc->njc/dot_general | solution.py:67
  218.0 7.0 %fusion.1 = f32[128,8192]{1,0:T(8,128)} fusion(bf16[4,64,128]{2,1,0:T(8,128)(2,1)S(1)} %fusion.22, bf16[4,64,8192]{2,0,1:T(4,128)(2,1)S(1)} %copy-done.3), kind=kOutput, calls=%fused_computation.6 | convolution fusion | flops 537919488 | bytes 8454144 | tf_op jit(solution)/shard_map/njc,njd->cd/dot_general | solution.py:87
  226.7 4.1 collective-permute-start.8
  230.8 43.7 %collective-permute-start.7 = (bf16[64,8192]{1,0:T(8,128)(2,1)S(1)}, bf16[64,8192]{1,0:T(8,128)(2,1)S(1)}, u32[]{:S(2)}, u32[]{:S(2)}) collective-permute-start(bf16[64,8192]{1,0:T(8,128)(2,1)S(1)} %get-tuple-element.16), channel_id=1, source_target_pairs={{0,6},{1,7},{2,0},{3,1},{4,2},{5,3},{6,4},{7,5},{8,14},{9,15},{10,... | collective-permute-start | bytes 3145736 | tf_op jit(solution)/shard_map/ppermute | solution.py:12
  276.4 5.5 %collective-permute-start.14 = (bf16[64,8192]{1,0:T(8,128)(2,1)S(1)}, bf16[64,8192]{1,0:T(8,128)(2,1)S(1)}, u32[]{:S(2)}, u32[]{:S(2)}) collective-permute-start(bf16[64,8192]{1,0:T(8,128)(2,1)S(1)} %get-tuple-element.7), channel_id=1, source_target_pairs={{0,5},{1,6},{2,7},{3,0},{4,1},{5,2},{6,3},{7,4},{8,13},{9,14},{10,... | collective-permute-start | bytes 3145736 | tf_op jit(solution)/shard_map/ppermute | solution.py:12
  281.9 15.5 %collective-permute-start.12 = (bf16[64,8192]{1,0:T(8,128)(2,1)S(1)}, bf16[64,8192]{1,0:T(8,128)(2,1)S(1)}, u32[]{:S(2)}, u32[]{:S(2)}) collective-permute-start(bf16[64,8192]{1,0:T(8,128)(2,1)S(1)} %get-tuple-element.9), channel_id=1, source_target_pairs={{0,7},{1,0},{2,1},{3,2},{4,3},{5,4},{6,5},{7,6},{8,15},{9,8},{10,9... | collective-permute-start | bytes 3145736 | tf_op jit(solution)/shard_map/ppermute | solution.py:12
  297.4 21.3 %collective-permute-done.7 = bf16[64,8192]{1,0:T(8,128)(2,1)S(1)} collective-permute-done((bf16[64,8192]{1,0:T(8,128)(2,1)S(1)}, bf16[64,8192]{1,0:T(8,128)(2,1)S(1)}, u32[]{:S(2)}, u32[]{:S(2)}) %collective-permute-start.7) | collective-permute-done | bytes 1048608 | tf_op jit(solution)/shard_map/ppermute | solution.py:12
  318.7 27.5 %collective-permute-done.6 = bf16[64,8192]{1,0:T(8,128)(2,1)S(1)} collective-permute-done((bf16[64,8192]{1,0:T(8,128)(2,1)S(1)}, bf16[64,8192]{1,0:T(8,128)(2,1)S(1)}, u32[]{:S(2)}, u32[]{:S(2)}) %collective-permute-start.6) | collective-permute-done | bytes 1048608 | tf_op jit(solution)/shard_map/ppermute | solution.py:12
  346.7 4.0 convolution_convert_fusion.4
  350.7 2.5 copy.62
  353.2 83.7 %collective-permute-done.14 = bf16[64,8192]{1,0:T(8,128)(2,1)S(1)} collective-permute-done((bf16[64,8192]{1,0:T(8,128)(2,1)S(1)}, bf16[64,8192]{1,0:T(8,128)(2,1)S(1)}, u32[]{:S(2)}, u32[]{:S(2)}) %collective-permute-start.14) | collective-permute-done | bytes 1048608 | tf_op jit(solution)/shard_map/ppermute | solution.py:12
  437.4 4.0 convolution_convert_fusion.3
  (66 shorter events, 35.0 us)
Async XLA Ops:
  7.2 181.1 %copy-start = (bf16[2,64,8192]{2,1,0:T(8,128)(2,1)S(1)}, bf16[2,64,8192]{2,1,0:T(8,128)(2,1)}, u32[]{:S(2)}) copy-start(bf16[2,64,8192]{2,1,0:T(8,128)(2,1)} %param.8) | copy-start | bytes 6291460
  7.2 436.8 %reduce-scatter.3.cloned.1.call-start = ((), (), s32[]{:S(2)}) async-start(), calls=%async_computation.2 | async-start | bytes 5242880 | tf_op jit(solution)/shard_map/reduce_scatter | solution.py:99
  8.8 45.4 %collective-permute-start.5 = (bf16[1]{0:T(256)(128)(2,1)}, bf16[1]{0:T(256)(128)(2,1)}, u32[]{:S(2)}, u32[]{:S(2)}) collective-permute-start(bf16[1]{0:T(256)(128)(2,1)} %get-tuple-element.23), channel_id=1, source_target_pairs={{0,3},{1,4},{2,5},{3,6},{4,7},{5,0},{6,1},{7,2},{8,11},{9,12},{10,... | collective-permute-start | bytes 14 | tf_op jit(solution)/shard_map/ppermute | solution.py:12
  8.8 46.7 %collective-permute-start.4 = (bf16[1]{0:T(256)(128)(2,1)}, bf16[1]{0:T(256)(128)(2,1)}, u32[]{:S(2)}, u32[]{:S(2)}) collective-permute-start(bf16[1]{0:T(256)(128)(2,1)} %get-tuple-element.24), channel_id=1, source_target_pairs={{0,2},{1,3},{2,4},{3,5},{4,6},{5,7},{6,0},{7,1},{8,10},{9,11},{10,... | collective-permute-start | bytes 14 | tf_op jit(solution)/shard_map/ppermute | solution.py:12
  11.0 46.6 %collective-permute-start.3 = (bf16[1]{0:T(256)(128)(2,1)}, bf16[1]{0:T(256)(128)(2,1)}, u32[]{:S(2)}, u32[]{:S(2)}) collective-permute-start(bf16[1]{0:T(256)(128)(2,1)} %get-tuple-element.25), channel_id=1, source_target_pairs={{0,1},{1,2},{2,3},{3,4},{4,5},{5,6},{6,7},{7,0},{8,9},{9,10},{10,1... | collective-permute-start | bytes 14 | tf_op jit(solution)/shard_map/ppermute | solution.py:12
  28.1 4.8 %copy-start.8 = (bf16[128,8192]{1,0:T(8,128)(2,1)S(1)}, bf16[128,8192]{1,0:T(8,128)(2,1)}, u32[]{:S(2)}) copy-start(bf16[128,8192]{1,0:T(8,128)(2,1)} %param.6) | copy-start | bytes 6291460
  29.2 29.7 %collective-permute-start = (bf16[64,8192]{1,0:T(8,128)(2,1)S(1)}, bf16[64,8192]{1,0:T(8,128)(2,1)S(1)}, u32[]{:S(2)}, u32[]{:S(2)}) collective-permute-start(bf16[64,8192]{1,0:T(8,128)(2,1)S(1)} %bitcast.92), channel_id=1, source_target_pairs={{0,1},{1,2},{2,3},{3,4},{4,5},{5,6},{6,7},{7,0},{8,9},{9,10},{10,1... | collective-permute-start | bytes 3145736 | tf_op jit(solution)/shard_map/ppermute | solution.py:12
  32.7 43.0 %collective-permute-start.1 = (bf16[64,8192]{1,0:T(8,128)(2,1)}, bf16[64,8192]{1,0:T(8,128)(2,1)}, u32[]{:S(2)}, u32[]{:S(2)}) collective-permute-start(bf16[64,8192]{1,0:T(8,128)(2,1)} %bitcast.80), channel_id=1, source_target_pairs={{0,2},{1,3},{2,4},{3,5},{4,6},{5,7},{6,0},{7,1},{8,10},{9,11},{10,... | collective-permute-start | bytes 3145736 | tf_op jit(solution)/shard_map/ppermute | solution.py:12
  54.2 42.3 %collective-permute-start.2 = (bf16[64,8192]{1,0:T(8,128)(2,1)}, bf16[64,8192]{1,0:T(8,128)(2,1)}, u32[]{:S(2)}, u32[]{:S(2)}) collective-permute-start(bf16[64,8192]{1,0:T(8,128)(2,1)} %bitcast.79), channel_id=1, source_target_pairs={{0,3},{1,4},{2,5},{3,6},{4,7},{5,0},{6,1},{7,2},{8,11},{9,12},{10,... | collective-permute-start | bytes 3145736 | tf_op jit(solution)/shard_map/ppermute | solution.py:12
  55.5 63.9 %collective-permute-start.9 = (bf16[64,8192]{1,0:T(8,128)(2,1)}, bf16[64,8192]{1,0:T(8,128)(2,1)}, u32[]{:S(2)}, u32[]{:S(2)}) collective-permute-start(bf16[64,8192]{1,0:T(8,128)(2,1)} %bitcast.78), channel_id=1, source_target_pairs={{0,1},{1,2},{2,3},{3,4},{4,5},{5,6},{6,7},{7,0},{8,9},{9,10},{10,1... | collective-permute-start | bytes 3145736 | tf_op jit(solution)/shard_map/ppermute | solution.py:12
  57.6 84.7 %collective-permute-start.10 = (bf16[64,8192]{1,0:T(8,128)(2,1)}, bf16[64,8192]{1,0:T(8,128)(2,1)}, u32[]{:S(2)}, u32[]{:S(2)}) collective-permute-start(bf16[64,8192]{1,0:T(8,128)(2,1)} %bitcast.77), channel_id=1, source_target_pairs={{0,2},{1,3},{2,4},{3,5},{4,6},{5,7},{6,0},{7,1},{8,10},{9,11},{10,... | collective-permute-start | bytes 3145736 | tf_op jit(solution)/shard_map/ppermute | solution.py:12
  58.9 1.0 copy-start.7
  58.9 105.3 %collective-permute-start.11 = (bf16[64,8192]{1,0:T(8,128)(2,1)S(1)}, bf16[64,8192]{1,0:T(8,128)(2,1)}, u32[]{:S(2)}, u32[]{:S(2)}) collective-permute-start(bf16[64,8192]{1,0:T(8,128)(2,1)S(1)} %bitcast.90), channel_id=1, source_target_pairs={{0,3},{1,4},{2,5},{3,6},{4,7},{5,0},{6,1},{7,2},{8,11},{9,12},{10,... | collective-permute-start | bytes 3145736 | tf_op jit(solution)/shard_map/ppermute | solution.py:12
  119.4 48.4 %copy-start.5 = (bf16[1,64,8192]{2,0,1:T(2,128)(2,1)S(1)}, bf16[1,64,8192]{2,0,1:T(2,128)(2,1)}, u32[]{:S(2)}) copy-start(bf16[1,64,8192]{2,0,1:T(2,128)(2,1)} %get-tuple-element.10) | copy-start | bytes 3145732
  188.3 4.9 %copy-start.2 = (bf16[4,64,8192]{2,0,1:T(4,128)(2,1)}, bf16[4,64,8192]{2,0,1:T(4,128)(2,1)S(1)}, u32[]{:S(2)}) copy-start(bf16[4,64,8192]{2,0,1:T(4,128)(2,1)S(1)} %pad_maximum_fusion.2) | copy-start | bytes 12582916
  188.3 4.9 %copy-start.4 = (bf16[1,64,8192]{2,0,1:T(2,128)(2,1)S(1)}, bf16[1,64,8192]{2,0,1:T(2,128)(2,1)}, u32[]{:S(2)}) copy-start(bf16[1,64,8192]{2,0,1:T(2,128)(2,1)} %get-tuple-element.18) | copy-start | bytes 3145732
  203.0 6.9 %copy-start.1 = (bf16[4,64,8192]{2,0,1:T(4,128)(2,1)}, bf16[4,64,8192]{2,0,1:T(4,128)(2,1)S(1)}, u32[]{:S(2)}) copy-start(bf16[4,64,8192]{2,0,1:T(4,128)(2,1)S(1)} %pad_maximum_fusion) | copy-start | bytes 12582916
  209.9 236.1 %reduce-scatter.5.cloned.1.call-start = ((), (), s32[]{:S(2)}) async-start(), calls=%async_computation.3 | async-start | bytes 5242880 | tf_op jit(solution)/shard_map/reduce_scatter | solution.py:100
  210.2 7.8 %copy-start.3 = (bf16[4,64,8192]{2,0,1:T(4,128)(2,1)S(1)}, bf16[4,64,8192]{2,0,1:T(4,128)(2,1)}, u32[]{:S(2)}) copy-start(bf16[4,64,8192]{2,0,1:T(4,128)(2,1)} %copy-done.2) | copy-start | bytes 12582916
  226.2 48.5 %copy-start.6 = (bf16[2,8192,64]{1,2,0:T(8,128)(2,1)S(1)}, bf16[2,8192,64]{1,2,0:T(8,128)(2,1)}, u32[]{:S(2)}) copy-start(bf16[2,8192,64]{1,2,0:T(8,128)(2,1)} %param.7) | copy-start | bytes 6291460
  226.7 55.2 %collective-permute-start.8 = (bf16[64,8192]{1,0:T(8,128)(2,1)S(1)}, bf16[64,8192]{1,0:T(8,128)(2,1)S(1)}, u32[]{:S(2)}, u32[]{:S(2)}) collective-permute-start(bf16[64,8192]{1,0:T(8,128)(2,1)S(1)} %get-tuple-element.15), channel_id=1, source_target_pairs={{0,5},{1,6},{2,7},{3,0},{4,1},{5,2},{6,3},{7,4},{8,13},{9,14},{10,... | collective-permute-start | bytes 3145736 | tf_op jit(solution)/shard_map/ppermute | solution.py:12
  230.8 87.9 %collective-permute-start.7 = (bf16[64,8192]{1,0:T(8,128)(2,1)S(1)}, bf16[64,8192]{1,0:T(8,128)(2,1)S(1)}, u32[]{:S(2)}, u32[]{:S(2)}) collective-permute-start(bf16[64,8192]{1,0:T(8,128)(2,1)S(1)} %get-tuple-element.16), channel_id=1, source_target_pairs={{0,6},{1,7},{2,0},{3,1},{4,2},{5,3},{6,4},{7,5},{8,14},{9,15},{10,... | collective-permute-start | bytes 3145736 | tf_op jit(solution)/shard_map/ppermute | solution.py:12
  274.5 71.7 %collective-permute-start.6 = (bf16[64,8192]{1,0:T(8,128)(2,1)S(1)}, bf16[64,8192]{1,0:T(8,128)(2,1)S(1)}, u32[]{:S(2)}, u32[]{:S(2)}) collective-permute-start(bf16[64,8192]{1,0:T(8,128)(2,1)S(1)} %get-tuple-element.17), channel_id=1, source_target_pairs={{0,7},{1,0},{2,1},{3,2},{4,3},{5,4},{6,5},{7,6},{8,15},{9,8},{10,9... | collective-permute-start | bytes 3145736 | tf_op jit(solution)/shard_map/ppermute | solution.py:12
  276.4 160.5 %collective-permute-start.14 = (bf16[64,8192]{1,0:T(8,128)(2,1)S(1)}, bf16[64,8192]{1,0:T(8,128)(2,1)S(1)}, u32[]{:S(2)}, u32[]{:S(2)}) collective-permute-start(bf16[64,8192]{1,0:T(8,128)(2,1)S(1)} %get-tuple-element.7), channel_id=1, source_target_pairs={{0,5},{1,6},{2,7},{3,0},{4,1},{5,2},{6,3},{7,4},{8,13},{9,14},{10,... | collective-permute-start | bytes 3145736 | tf_op jit(solution)/shard_map/ppermute | solution.py:12
  281.9 155.0 %collective-permute-start.13 = (bf16[64,8192]{1,0:T(8,128)(2,1)S(1)}, bf16[64,8192]{1,0:T(8,128)(2,1)S(1)}, u32[]{:S(2)}, u32[]{:S(2)}) collective-permute-start(bf16[64,8192]{1,0:T(8,128)(2,1)S(1)} %get-tuple-element.8), channel_id=1, source_target_pairs={{0,6},{1,7},{2,0},{3,1},{4,2},{5,3},{6,4},{7,5},{8,14},{9,15},{10,... | collective-permute-start | bytes 3145736 | tf_op jit(solution)/shard_map/ppermute | solution.py:12
  281.9 155.0 %collective-permute-start.12 = (bf16[64,8192]{1,0:T(8,128)(2,1)S(1)}, bf16[64,8192]{1,0:T(8,128)(2,1)S(1)}, u32[]{:S(2)}, u32[]{:S(2)}) collective-permute-start(bf16[64,8192]{1,0:T(8,128)(2,1)S(1)} %get-tuple-element.9), channel_id=1, source_target_pairs={{0,7},{1,0},{2,1},{3,2},{4,3},{5,4},{6,5},{7,6},{8,15},{9,8},{10,9... | collective-permute-start | bytes 3145736 | tf_op jit(solution)/shard_map/ppermute | solution.py:12
Sparse Core Ops, SparseCore 0:
  210.1 92.8 reduce-scatter.2
  305.7 44.5 reduce-scatter.4
where the time goes:
time: 460 us; the launch traced here: 455 us
  waiting for transfers between devices  216 us (47%)
  starting transfers between devices  79.4 us (17%)
  local copies, waits for them, and re-layouts  59.5 us (13%)
  matrix products  46.5 us (10%)
  other arithmetic  39.1 us (8%)
  between operations  14.8 us (3%)
    ppermute x15, waiting for transfers between devices, shifted(): return lax.ppermute(value, axis, pairs)  216 us
    ppermute x15, starting transfers between devices, shifted(): return lax.ppermute(value, axis, pairs)  79.1 us
    another operation x1, other arithmetic, on_device(): arrived_grads = jnp.stack(grads_list)  20.5 us
    unnamed x24, local copies, waits for them, and re-layouts  11.4 us
    another operation x3, local copies, waits for them, and re-layouts, on_device(): arrived_grads = jnp.stack(grads_list)  10.8 us
    another operation x3, local copies, waits for them, and re-layouts, on_device(): arrived_rows = jnp.stack(rows_list)  10.6 us
    slice x1, local copies, waits for them, and re-layouts, on_device(): rows_list = [sent_rows[slot_index] for slot_index in range(reach_count)]  10 us
    slice x1, local copies, waits for them, and re-layouts, on_device(): grads_list = [sent_grads[slot_index] for slot_index in range(reach_count)]  10 us
  transfers between devices with their start and end apart: 17, of which 8 were waited for; matrix products, arithmetic and copies ran while one was open for 21% of the time, Pallas kernels for 0%

commit v1 on v0

v1 whole, which is shorter than its diff:
```python
import functools

import jax
import jax.numpy as jnp
from jax import lax
from jax.experimental import pallas as pl
from jax.experimental.pallas import tpu as pltpu
from jax.sharding import PartitionSpec as P

MESH = pl.DeviceIdType.MESH
scale = 2.0


def step_kernel(
    n, groups, segs, rank, reach,
    tokens, grads, pack, mask, out, gtok, gdown, gup,
    X, G, PP, M, HP, HR, HG, Hm, Gm, OB, TB, C, RA, RB, RC, RF, S1, S2, S3,
    loc, a2a_s, a2a_r, pan_s, pan_r, hp_s, hp_r, hg_s, hg_r, ob_s, ob_r,
    g_s, ra_r, rb_r, rc_r, rf_r,
):
    T, D = tokens.shape
    W = D // n
    B = PP.shape[2]
    seg_rows = T // segs
    nb = n // 2
    me = lax.axis_index("dp")
    j = lax.axis_index("adapter")
    blk, core = me // 2, me % 2
    y = j % 2
    mate = j + 1 - 2 * y
    up2, down2 = (j + 2) % groups, (j + groups - 2) % groups

    offsets = [(u, v) for u in range(1, nb) for v in range(2)] + [(0, 1)]
    peers = [(((blk + u) % nb) * 2 + (core + v) % 2) for u, v in offsets]
    senders = [(((blk + nb - u) % nb) * 2 + (core + v) % 2) for u, v in offsets]
    np_ = len(offsets)

    def rows(p):
        return pl.ds(pl.multiple_of(p * T, T), T)

    def cols(p):
        return pl.ds(pl.multiple_of(p * W, W), W)

    def rcopy(src, dst, s, r, **dev):
        return pltpu.make_async_remote_copy(
            src_ref=src, dst_ref=dst, send_sem=s, recv_sem=r, device_id=dev, device_id_type=MESH
        )

    barrier = pltpu.get_barrier_semaphore()
    for p in peers:
        pl.semaphore_signal(barrier, inc=1, device_id={"dp": p}, device_id_type=MESH)
    for h in (mate, up2, down2):
        pl.semaphore_signal(barrier, inc=1, device_id={"adapter": h}, device_id_type=MESH)
    pl.semaphore_wait(barrier, np_ + 3)

    for c in range(2):
        rcopy(pack.at[c], PP.at[c, 2], pan_s.at[0, c], pan_r.at[2, c], adapter=down2).start()

    @pl.when(y == 1)
    def _():
        for c in range(2):
            rcopy(pack.at[c], PP.at[c, 1], pan_s.at[1, c], pan_r.at[1, c], adapter=mate).start()

    for i, p in enumerate(peers):
        rcopy(mask, M.at[me], a2a_s.at[2, i], a2a_r.at[2, i], dp=p).start()
    for c, (src, dst) in enumerate(((tokens, X), (grads, G))):
        for i, p in enumerate(peers):
            rcopy(src.at[:, cols(p)], dst.at[rows(me)], a2a_s.at[c, i], a2a_r.at[c, i], dp=p).start()
    locals_ = [
        pltpu.make_async_copy(tokens.at[:, cols(me)], X.at[rows(me)], loc.at[0]),
        pltpu.make_async_copy(grads.at[:, cols(me)], G.at[rows(me)], loc.at[1]),
        pltpu.make_async_copy(pack.at[0], PP.at[0, 0], loc.at[2]),
        pltpu.make_async_copy(pack.at[1], PP.at[1, 0], loc.at[3]),
        pltpu.make_async_copy(mask, M.at[me], loc.at[4]),
    ]
    for cp in locals_:
        cp.start()
    for cp in locals_:
        cp.wait()

    def pan_wait(slot, c):
        rcopy(pack.at[c], PP.at[c, slot], pan_s.at[0, c], pan_r.at[slot, c], adapter=down2).wait_recv()

    for c in range(2):
        pan_wait(2, c)

        @pl.when(y == 0)
        def _():
            rcopy(PP.at[c, 2], PP.at[c, 1], pan_s.at[2, c], pan_r.at[1, c], adapter=mate).start()

        @pl.when(y == 1)
        def _():
            rcopy(PP.at[c, 2], PP.at[c, 3], pan_s.at[2, c], pan_r.at[3, c], adapter=mate).start()

    for c in range(2):
        pan_wait(1, c)

        @pl.when(y == 1)
        def _():
            rcopy(PP.at[c, 1], PP.at[c, 3], pan_s.at[3, c], pan_r.at[3, c], adapter=down2).start()

    for i in range(np_):
        s = senders[i]
        rcopy(mask, M.at[s], a2a_s.at[2, i], a2a_r.at[2, i], dp=peers[i]).wait_recv()
        for c, (src, dst) in enumerate(((tokens, X), (grads, G))):
            rcopy(src.at[:, cols(me)], dst.at[rows(s)], a2a_s.at[c, i], a2a_r.at[c, i], dp=peers[i]).wait_recv()

    lane = lax.broadcasted_iota(jnp.int32, (T, B), 1)
    low = lane < rank

    def row_mask(p):
        m = M[p]
        return jnp.concatenate(
            [jnp.broadcast_to(m[s:s + 1], (seg_rows, reach * B)) for s in range(segs)], axis=0
        )

    def fold(full, m):
        full = full * m
        acc = full[:, 0:B]
        for k in range(1, reach):
            acc = acc + full[:, k * B:(k + 1) * B]
        return acc + pltpu.roll(acc, rank, 1)

    nt = (((1,), (1,)), ((), ()))

    def part_dot(src, c, p):
        return lax.dot_general(
            src[rows(p), :], PP[c].reshape(reach * B, W), nt, preferred_element_type=jnp.float32
        )

    pan_wait(3, 0)

    @pl.loop(0, n)
    def _(p):
        HP[p] = fold(part_dot(X, 0, p), row_mask(p))

    pan_wait(3, 1)

    @pl.loop(0, n)
    def _(p):
        HP[p] = jnp.where(low, HP[p], scale * fold(part_dot(G, 1, p), row_mask(p)))

    for i, p in enumerate(peers):
        rcopy(HP.at[p], HR.at[me], hp_s.at[i], hp_r.at[i], dp=p).start()
    total = HP[me]
    for i in range(np_):
        s = senders[i]
        rcopy(HP.at[me], HR.at[s], hp_s.at[i], hp_r.at[i], dp=peers[i]).wait_recv()
        total = total + HR[s]
    HG[me] = total.astype(jnp.bfloat16)
    for i, p in enumerate(peers):
        rcopy(HG.at[me], HG.at[me], hg_s.at[i], hg_r.at[i], dp=p).start()
    for i in range(np_):
        s = senders[i]
        rcopy(HG.at[s], HG.at[s], hg_s.at[i], hg_r.at[i], dp=peers[i]).wait_recv()

    @pl.loop(0, n)
    def _(p):
        hg = HG[p].astype(jnp.float32)
        other = pltpu.roll(hg, rank, 1)
        h = jnp.where(low, hg, other)
        g = jnp.where(low, other, hg)
        m = row_mask(p)
        Hm[rows(p), :] = (jnp.concatenate([h] * reach, axis=1) * m).astype(jnp.bfloat16)
        Gm[rows(p), :] = (jnp.concatenate([g] * reach, axis=1) * m).astype(jnp.bfloat16)

    tile = min(W, 512)
    tn = (((0,), (0,)), ((), ()))

    def contribution(k):
        ks = slice(k * B, (k + 1) * B)

        @pl.loop(0, W // tile)
        def _(t):
            at = pl.ds(pl.multiple_of(t * tile, tile), tile)
            C[k, 0, :, at] = lax.dot_general(Gm[:, ks], X[:, at], tn, preferred_element_type=jnp.float32)
            C[k, 1, :, at] = scale * lax.dot_general(
                Hm[:, ks], G[:, at], tn, preferred_element_type=jnp.float32
            )

    def outputs(p):
        @pl.loop(0, W // tile)
        def _(t):
            at = pl.ds(pl.multiple_of(t * tile, tile), tile)
            OB[rows(p), at] = (
                scale
                * jnp.dot(
                    Hm[rows(p), :], PP[1, :, :, at].reshape(reach * B, tile),
                    preferred_element_type=jnp.float32,
                )
            ).astype(jnp.bfloat16)
            TB[rows(p), at] = jnp.dot(
                Gm[rows(p), :], PP[0, :, :, at].reshape(reach * B, tile),
                preferred_element_type=jnp.float32,
            ).astype(jnp.bfloat16)

    def send_outputs(i):
        p = peers[i]
        rcopy(OB.at[rows(p)], out.at[:, cols(me)], ob_s.at[0, i], ob_r.at[0, i], dp=p).start()
        rcopy(TB.at[rows(p)], gtok.at[:, cols(me)], ob_s.at[1, i], ob_r.at[1, i], dp=p).start()

    contribution(3)
    for c in range(2):
        S3[c] = C[3, c].astype(jnp.bfloat16)

        @pl.when(y == 0)
        def _():
            rcopy(S3.at[c], RB.at[c], g_s.at[2, c], rb_r.at[c], adapter=mate).start()

        @pl.when(y == 1)
        def _():
            rcopy(S3.at[c], RA.at[c], g_s.at[2, c], ra_r.at[c], adapter=up2).start()

    outputs(peers[0])
    send_outputs(0)
    contribution(1)

    @pl.when(y == 0)
    def _():
        for c in range(2):
            S1[c] = C[1, c].astype(jnp.bfloat16)
            rcopy(S1.at[c], RC.at[c], g_s.at[0, c], rc_r.at[c], adapter=mate).start()

    for i in range(1, np_ - 1):
        outputs(peers[i])
        send_outputs(i)
    contribution(2)

    def wait_in(ref, sem, c):
        rcopy(S3.at[c], ref.at[c], g_s.at[2, c], sem.at[c], adapter=mate).wait_recv()

    @pl.when(y == 1)
    def _():
        for c in range(2):
            wait_in(RA, ra_r, c)
            S1[c] = (C[1, c] + RA[c].astype(jnp.float32)).astype(jnp.bfloat16)
            rcopy(S1.at[c], RA.at[c], g_s.at[0, c], ra_r.at[c], adapter=mate).start()

        for c in range(2):
            wait_in(RB, rb_r, c)
            S2[c] = (C[2, c] + RB[c].astype(jnp.float32)).astype(jnp.bfloat16)
            rcopy(S2.at[c], RF.at[c], g_s.at[1, c], rf_r.at[c], adapter=up2).start()

    outputs(peers[np_ - 1])
    send_outputs(np_ - 1)
    outputs(me)
    own = [
        pltpu.make_async_copy(OB.at[rows(me)], out.at[:, cols(me)], loc.at[0]),
        pltpu.make_async_copy(TB.at[rows(me)], gtok.at[:, cols(me)], loc.at[1]),
    ]
    for cp in own:
        cp.start()
    contribution(0)

    @pl.when(y == 0)
    def _():
        for c in range(2):
            wait_in(RA, ra_r, c)
            S2[c] = (C[2, c] + RA[c].astype(jnp.float32)).astype(jnp.bfloat16)
            rcopy(S2.at[c], RF.at[c], g_s.at[1, c], rf_r.at[c], adapter=up2).start()

    @pl.when(y == 1)
    def _():
        for c in range(2):
            wait_in(RC, rc_r, c)
            C[0, c] = C[0, c] + RC[c].astype(jnp.float32)

    for c, ref in enumerate((gdown, gup)):
        wait_in(RF, rf_r, c)
        ref[...] = (C[0, c] + RF[c].astype(jnp.float32)).astype(jnp.bfloat16)

    for cp in own:
        cp.wait()
    for i, p in enumerate(peers):
        s = senders[i]
        for c, (buf, dst) in enumerate(((OB, out), (TB, gtok))):
            cp = rcopy(buf.at[rows(p)], dst.at[:, cols(s)], ob_s.at[c, i], ob_r.at[c, i], dp=p)
            cp.wait_recv()
            cp.wait_send()
        rcopy(mask, M.at[me], a2a_s.at[2, i], a2a_r.at[2, i], dp=p).wait_send()
        for c, (src, dst) in enumerate(((tokens, X), (grads, G))):
            rcopy(src.at[:, cols(p)], dst.at[rows(me)], a2a_s.at[c, i], a2a_r.at[c, i], dp=p).wait_send()
        rcopy(HP.at[p], HR.at[me], hp_s.at[i], hp_r.at[i], dp=p).wait_send()
        rcopy(HG.at[me], HG.at[me], hg_s.at[i], hg_r.at[i], dp=p).wait_send()
    for c in range(2):
        rcopy(pack.at[c], PP.at[c, 2], pan_s.at[0, c], pan_r.at[2, c], adapter=down2).wait_send()
        rcopy(PP.at[c, 2], PP.at[c, 1], pan_s.at[2, c], pan_r.at[1, c], adapter=mate).wait_send()

        @pl.when(y == 1)
        def _():
            rcopy(pack.at[c], PP.at[c, 1], pan_s.at[1, c], pan_r.at[1, c], adapter=mate).wait_send()
            rcopy(PP.at[c, 1], PP.at[c, 3], pan_s.at[3, c], pan_r.at[3, c], adapter=down2).wait_send()

        for k, buf in enumerate((S1, S2, S3)):
            rcopy(buf.at[c], RF.at[c], g_s.at[k, c], rf_r.at[c], adapter=up2).wait_send()


def on_device(n, groups, tokens, grad_out, down_panels, up_panels, seg_adapter):
    held, D, rank = down_panels.shape
    segs = seg_adapter.shape[0]
    reach = 2 * segs
    T = tokens.shape[0]
    W = D // n
    B = held * rank
    me = lax.axis_index("dp")
    position = lax.axis_index("adapter")
    down_mine = lax.dynamic_slice_in_dim(down_panels, me * W, W, 1)
    up_mine = lax.dynamic_slice_in_dim(up_panels, me * W, W, 2)
    pack = jnp.stack([jnp.transpose(down_mine, (0, 2, 1)).reshape(B, W), up_mine.reshape(B, W)])
    owner = seg_adapter // held
    pick = jnp.mod(owner - position, groups) * held + seg_adapter - owner * held
    mask = (jnp.arange(reach * B, dtype=jnp.int32)[None, :] // rank == pick[:, None]).astype(jnp.float32)
    mask = jnp.pad(mask, ((0, -segs % 8), (0, 0)))

    any_ = pl.BlockSpec(memory_space=pl.ANY)
    vmem = pl.BlockSpec(memory_space=pltpu.VMEM)
    bf, f32 = jnp.bfloat16, jnp.float32
    dma = pltpu.SemaphoreType.DMA
    k = n - 1
    rows = n * T
    result = pl.pallas_call(
        functools.partial(step_kernel, n, groups, segs, rank, reach),
        out_shape=(
            jax.ShapeDtypeStruct((T, D), bf),
            jax.ShapeDtypeStruct((T, D), bf),
            jax.ShapeDtypeStruct((B, W), bf),
            jax.ShapeDtypeStruct((B, W), bf),
        ),
        in_specs=[any_, any_, any_, vmem],
        out_specs=(any_, any_, vmem, vmem),
        scratch_shapes=[
            pltpu.VMEM((rows, W), bf),
            pltpu.VMEM((rows, W), bf),
            pltpu.VMEM((2, reach, B, W), bf),
            pltpu.VMEM((n,) + mask.shape, f32),
            pltpu.VMEM((n, T, B), f32),
            pltpu.VMEM((n, T, B), f32),
            pltpu.VMEM((n, T, B), bf),
            pltpu.VMEM((rows, reach * B), bf),
            pltpu.VMEM((rows, reach * B), bf),
            pltpu.VMEM((rows, W), bf),
            pltpu.VMEM((rows, W), bf),
            pltpu.VMEM((reach, 2, B, W), f32),
        ]
        + [pltpu.VMEM((2, B, W), bf)] * 7
        + [
            dma((5,)), dma((3, k)), dma((3, k)), dma((4, 2)), dma((4, 2)),
            dma((k,)), dma((k,)), dma((k,)), dma((k,)), dma((2, k)), dma((2, k)),
            dma((3, 2)), dma((2,)), dma((2,)), dma((2,)), dma((2,)),
        ],
        compiler_params=pltpu.CompilerParams(
            collective_id=0, has_side_effects=True, vmem_limit_bytes=50 * 1024 * 1024
        ),
        cost_estimate=pl.CostEstimate(
            flops=12 * rows * W * reach * B, bytes_accessed=16 * 2 ** 20, transcendentals=0
        ),
    )(tokens, grad_out, pack, mask)
    out, gtok, gdown, gup = result
    gdown = jnp.transpose(gdown.reshape(held, rank, W), (0, 2, 1))
    return out, gtok, gdown, gup.reshape(held, rank, W)


def solution(mesh):
    placed = (
        P(("dp", "adapter"), None),
        P(("dp", "adapter"), None),
        P("adapter", None, None),
        P("adapter", None, None),
        P(("dp", "adapter")),
    )
    return jax.shard_map(
        functools.partial(on_device, mesh.shape["dp"], mesh.shape["adapter"]),
        mesh=mesh,
        in_specs=placed,
        out_specs=(
            P(("dp", "adapter"), None),
            P(("dp", "adapter"), None),
            P("adapter", "dp", None),
            P("adapter", None, "dp"),
        ),
        check_vma=False,
    )
```

time: 460 us -> 130 us (0.28)
  the two profiles are of different devices: /device:TPU:29 before, /device:TPU:0 now
where the time goes in v1:
time: 130 us
  Pallas kernels  120 us (92%)
  local copies, waits for them, and re-layouts  7.95 us (6%)
    pallas_call x1, Pallas kernels, on_device(): pl.pallas_call(functools.partial(step_kernel, n, groups, segs, rank, reac...  120 us
    unnamed x8, local copies, waits for them, and re-layouts  6.84 us

profile of v1, /device:TPU:0, one launch (start us, length us, event | category | flops | bytes accessed | tf_op | source)
XLA Modules:
  0.0 129.7 jit_solution(7595952939964007373)
XLA Ops:
  0.6 0.0 copy-start
  0.7 0.8 fusion.5
  1.5 0.1 broadcast_compare_fusion
  1.6 0.7 copy-done
  2.3 1.1 constant_dynamic-slice_fusion
  3.4 0.1 pad_maximum_fusion.pack
  3.5 120.1 %shard_map.84 = (bf16[128,8192]{1,0:T(8,128)(2,1)}, bf16[128,8192]{1,0:T(8,128)(2,1)}, bf16[128,2048]{1,0:T(8,128)(2,1)S(1)}, bf16[128,2048]{1,0:T(8,128)(2,1)S(1)}) custom-call(bf16[128,8192]{1,0:T(8,128)(2,1)} %tokens.1, bf16[128,8192]{1,0:T(8,128)(2,1)} %grads.1, bf16[2,128,2048]{2,1,0:T(8,128)(2,1)S(1)} %pad_maximum_fusion.pack, ...), custom_call_target="tpu_custom_call" | custom-call | flops 6442450944 | bytes 16777216 | tf_op jit(solution)/shard_map/pallas_call | solution.py:321
  123.6 0.0 copy-start.1
  123.6 3.2 %copy.13 = bf16[128,8192]{1,0:T(8,128)(2,1)} copy(bf16[128,8192]{1,0:T(8,128)(2,1)} %get-tuple-element.16) | data formatting | bytes 4194304
  126.8 0.0 copy-done.1
  126.8 1.3 %copy.14 = bf16[128,8192]{1,0:T(8,128)(2,1)} copy(bf16[128,8192]{1,0:T(8,128)(2,1)S(1)} %copy-done.1) | data formatting | bytes 4194304
  128.1 0.8 copy.15
  128.9 0.8 copy.16
  (3 shorter events, 0.0 us)
Async XLA Ops:
  0.6 1.6 %copy-start = (bf16[2,8192,64]{1,2,0:T(8,128)(2,1)S(1)}, bf16[2,8192,64]{1,2,0:T(8,128)(2,1)}, u32[]{:S(2)}) copy-start(bf16[2,8192,64]{1,2,0:T(8,128)(2,1)} %param.7) | copy-start | bytes 6291460
  123.6 3.3 %copy-start.1 = (bf16[128,8192]{1,0:T(8,128)(2,1)S(1)}, bf16[128,8192]{1,0:T(8,128)(2,1)}, u32[]{:S(2)}) copy-start(bf16[128,8192]{1,0:T(8,128)(2,1)} %get-tuple-element.17) | copy-start | bytes 6291460

commit v2 on v1

v2 whole, which is shorter than its diff:
```python
import functools

import jax
import jax.numpy as jnp
from jax import lax
from jax.experimental import pallas as pl
from jax.experimental.pallas import tpu as pltpu
from jax.sharding import PartitionSpec as P

MESH = pl.DeviceIdType.MESH
scale = 2.0


def step_kernel(
    n, groups, segs, rank, reach,
    tokens, grads, down, up, mask, out, gtok, gdown, gup,
    X, G, PP, M, HP, HR, HG, Hm, Gm, OB, TB, C, RA, RB, RC, RF, S1, S2, S3,
    loc, a2a_s, a2a_r, pan_s, pan_r, hp_s, hp_r, hg_s, hg_r, ob_s, ob_r,
    g_s, ra_r, rb_r, rc_r, rf_r,
):
    T, D = tokens.shape
    W = D // n
    B = PP.shape[2]
    seg_rows = T // segs
    nb = n // 2
    me = lax.axis_index("dp")
    j = lax.axis_index("adapter")
    blk, core = me // 2, me % 2
    y = j % 2
    mate = j + 1 - 2 * y
    up2, down2 = (j + 2) % groups, (j + groups - 2) % groups

    offsets = [(u, v) for u in range(1, nb) for v in range(2)] + [(0, 1)]
    peers = [(((blk + u) % nb) * 2 + (core + v) % 2) for u, v in offsets]
    senders = [(((blk + nb - u) % nb) * 2 + (core + v) % 2) for u, v in offsets]
    np_ = len(offsets)

    def rows(p):
        return pl.ds(pl.multiple_of(p * T, T), T)

    def cols(p):
        return pl.ds(pl.multiple_of(p * W, W), W)

    def rcopy(src, dst, s, r, **dev):
        return pltpu.make_async_remote_copy(
            src_ref=src, dst_ref=dst, send_sem=s, recv_sem=r, device_id=dev, device_id_type=MESH
        )

    barrier = pltpu.get_barrier_semaphore()
    for p in peers:
        pl.semaphore_signal(barrier, inc=1, device_id={"dp": p}, device_id_type=MESH)
    for h in (mate, up2, down2):
        pl.semaphore_signal(barrier, inc=1, device_id={"adapter": h}, device_id_type=MESH)
    pl.semaphore_wait(barrier, np_ + 3)

    half = B // 2
    quarters = range(4)

    def part(ref, q, slot=None):
        at = pl.ds((q % 2) * half, half)
        return ref[q // 2].at[at, cols(me)] if slot is None else ref.at[q // 2, slot, at]

    panels = (down, up)

    def own_down(q):
        return rcopy(part(panels, q), part(PP, q, 2), pan_s.at[0, q], pan_r.at[2, q], adapter=down2)

    def own_mate(q):
        return rcopy(part(panels, q), part(PP, q, 1), pan_s.at[1, q], pan_r.at[1, q], adapter=mate)

    def relay_mate(q, slot):
        return rcopy(part(PP, q, 2), part(PP, q, slot), pan_s.at[2, q], pan_r.at[slot, q], adapter=mate)

    def relay_down(q):
        return rcopy(part(PP, q, 1), part(PP, q, 3), pan_s.at[3, q], pan_r.at[3, q], adapter=down2)

    def pan_wait(slot, q):
        rcopy(part(PP, q, 0), part(PP, q, slot), pan_s.at[0, q], pan_r.at[slot, q], adapter=down2).wait_recv()

    for q in (0, 1):
        own_down(q).start()

    @pl.when(y == 0)
    def _():
        for q in (2, 3):
            own_down(q).start()

    @pl.when(y == 1)
    def _():
        for q in (0, 1):
            own_mate(q).start()

    for i, p in enumerate(peers):
        rcopy(mask, M.at[me], a2a_s.at[2, i], a2a_r.at[2, i], dp=p).start()
    for c, (src, dst) in enumerate(((tokens, X), (grads, G))):
        for i, p in enumerate(peers):
            rcopy(src.at[:, cols(p)], dst.at[rows(me)], a2a_s.at[c, i], a2a_r.at[c, i], dp=p).start()
    locals_ = [
        pltpu.make_async_copy(tokens.at[:, cols(me)], X.at[rows(me)], loc.at[0]),
        pltpu.make_async_copy(grads.at[:, cols(me)], G.at[rows(me)], loc.at[1]),
        pltpu.make_async_copy(down.at[:, cols(me)], PP.at[0, 0], loc.at[2]),
        pltpu.make_async_copy(up.at[:, cols(me)], PP.at[1, 0], loc.at[3]),
        pltpu.make_async_copy(mask, M.at[me], loc.at[4]),
    ]
    for cp in locals_:
        cp.start()
    for cp in locals_:
        cp.wait()

    for c in range(2):
        for q in (2 * c, 2 * c + 1):
            pan_wait(2, q)

            @pl.when(y == 0)
            def _():
                relay_mate(q, 1).start()

            @pl.when(y == 1)
            def _():
                relay_mate(q, 3).start()

        for q in (2 * c, 2 * c + 1):
            pan_wait(1, q)

            @pl.when(y == 1)
            def _():
                relay_down(q).start()
                if c == 0:
                    own_down(q + 2).start()
                    own_mate(q + 2).start()

    lane_rows = reach * B

    def row_mask(p):
        m = M[p]
        return jnp.concatenate(
            [jnp.broadcast_to(m[s:s + 1], (seg_rows, lane_rows)) for s in range(segs)], axis=0
        )

    def fold(full, m):
        full = full * m
        acc = full[:, 0:B]
        for k in range(1, reach):
            acc = acc + full[:, k * B:(k + 1) * B]
        return acc + pltpu.roll(acc, rank, 1)

    nt = (((1,), (1,)), ((), ()))

    def rows_wait(c):
        src, dst = ((tokens, X), (grads, G))[c]
        for i in range(np_):
            rcopy(
                src.at[:, cols(me)], dst.at[rows(senders[i])], a2a_s.at[c, i], a2a_r.at[c, i], dp=peers[i]
            ).wait_recv()

    def send_partials(c):
        src = (X, G)[c]

        @pl.loop(0, n)
        def _(p):
            full = lax.dot_general(
                src[rows(p), :], PP[c].reshape(reach * B, W), nt, preferred_element_type=jnp.float32
            )
            HP[c, p] = (1.0, scale)[c] * fold(full, row_mask(p))

        for i, p in enumerate(peers):
            rcopy(HP.at[c, p], HR.at[c, me], hp_s.at[c, i], hp_r.at[c, i], dp=p).start()

    def send_sums(c):
        total = HP[c, me]
        for i in range(np_):
            s = senders[i]
            rcopy(HP.at[c, me], HR.at[c, s], hp_s.at[c, i], hp_r.at[c, i], dp=peers[i]).wait_recv()
            total = total + HR[c, s]
        HG[c, me] = total.astype(jnp.bfloat16)
        for i, p in enumerate(peers):
            rcopy(HG.at[c, me], HG.at[c, me], hg_s.at[c, i], hg_r.at[c, i], dp=p).start()

    def spread(c):
        for i in range(np_):
            s = senders[i]
            rcopy(HG.at[c, s], HG.at[c, s], hg_s.at[c, i], hg_r.at[c, i], dp=peers[i]).wait_recv()
        wide = (Hm, Gm)[c]

        @pl.loop(0, n)
        def _(p):
            h = HG[c, p].astype(jnp.float32)
            wide[rows(p), :] = (jnp.concatenate([h] * reach, axis=1) * row_mask(p)).astype(jnp.bfloat16)

    tile = min(W, 512)
    tn = (((0,), (0,)), ((), ()))

    def contribution(c, k):
        ks = slice(k * B, (k + 1) * B)
        wide, src = ((Gm, X), (Hm, G))[c]

        @pl.loop(0, W // tile)
        def _(t):
            at = pl.ds(pl.multiple_of(t * tile, tile), tile)
            C[k, c, :, at] = (1.0, scale)[c] * lax.dot_general(
                wide[:, ks], src[:, at], tn, preferred_element_type=jnp.float32
            )

    def outputs(c, p):
        wide, buf = ((Gm, TB), (Hm, OB))[c]

        @pl.loop(0, W // tile)
        def _(t):
            at = pl.ds(pl.multiple_of(t * tile, tile), tile)
            buf[rows(p), at] = (
                (1.0, scale)[c]
                * jnp.dot(
                    wide[rows(p), :], PP[c, :, :, at].reshape(reach * B, tile),
                    preferred_element_type=jnp.float32,
                )
            ).astype(jnp.bfloat16)

    def output_copy(c, i, at):
        buf, dst = ((TB, gtok), (OB, out))[c]
        p = peers[i]
        return rcopy(buf.at[rows(p)], dst.at[:, cols(at)], ob_s.at[c, i], ob_r.at[c, i], dp=p)

    def send_outputs(c, i):
        outputs(c, peers[i])
        output_copy(c, i, me).start()

    def own_outputs(c):
        buf, dst = ((TB, gtok), (OB, out))[c]
        outputs(c, me)
        return pltpu.make_async_copy(buf.at[rows(me)], dst.at[:, cols(me)], loc.at[c])

    def wait_in(ref, sem, c):
        rcopy(S3.at[c], ref.at[c], g_s.at[2, c], sem.at[c], adapter=mate).wait_recv()

    def start_far(c):
        contribution(c, 3)
        S3[c] = C[3, c].astype(jnp.bfloat16)

        @pl.when(y == 0)
        def _():
            rcopy(S3.at[c], RB.at[c], g_s.at[2, c], rb_r.at[c], adapter=mate).start()

        @pl.when(y == 1)
        def _():
            rcopy(S3.at[c], RA.at[c], g_s.at[2, c], ra_r.at[c], adapter=up2).start()

    def start_near(c):
        contribution(c, 1)

        @pl.when(y == 0)
        def _():
            S1[c] = C[1, c].astype(jnp.bfloat16)
            rcopy(S1.at[c], RC.at[c], g_s.at[0, c], rc_r.at[c], adapter=mate).start()

    def relay_odd(c):
        @pl.when(y == 1)
        def _():
            wait_in(RA, ra_r, c)
            S1[c] = (C[1, c] + RA[c].astype(jnp.float32)).astype(jnp.bfloat16)
            rcopy(S1.at[c], RA.at[c], g_s.at[0, c], ra_r.at[c], adapter=mate).start()
            wait_in(RB, rb_r, c)
            S2[c] = (C[2, c] + RB[c].astype(jnp.float32)).astype(jnp.bfloat16)
            rcopy(S2.at[c], RF.at[c], g_s.at[1, c], rf_r.at[c], adapter=up2).start()

    def relay_even(c):
        @pl.when(y == 0)
        def _():
            wait_in(RA, ra_r, c)
            S2[c] = (C[2, c] + RA[c].astype(jnp.float32)).astype(jnp.bfloat16)
            rcopy(S2.at[c], RF.at[c], g_s.at[1, c], rf_r.at[c], adapter=up2).start()

    for i in range(np_):
        rcopy(mask, M.at[senders[i]], a2a_s.at[2, i], a2a_r.at[2, i], dp=peers[i]).wait_recv()
    rows_wait(0)
    for q in (0, 1):
        pan_wait(3, q)
    send_partials(0)
    send_sums(0)
    spread(0)

    rows_wait(1)
    for q in (2, 3):
        pan_wait(3, q)
    send_partials(1)
    start_far(1)
    for i in range(np_ - 1):
        send_outputs(1, i)
    send_sums(1)
    start_near(1)
    send_outputs(1, np_ - 1)
    contribution(1, 2)
    spread(1)
    start_far(0)
    for i in range(np_ - 1):
        send_outputs(0, i)
    start_near(0)
    relay_odd(1)
    send_outputs(0, np_ - 1)
    contribution(0, 2)
    own = [own_outputs(1)]
    own[0].start()
    contribution(1, 0)
    relay_even(1)
    own.append(own_outputs(0))
    own[1].start()
    contribution(0, 0)
    relay_odd(0)
    relay_even(0)

    @pl.when(y == 1)
    def _():
        for c in (1, 0):
            wait_in(RC, rc_r, c)
            C[0, c] = C[0, c] + RC[c].astype(jnp.float32)

    for c, ref in ((1, gup), (0, gdown)):
        wait_in(RF, rf_r, c)
        ref[...] = (C[0, c] + RF[c].astype(jnp.float32)).astype(jnp.bfloat16)

    for cp in own:
        cp.wait()
    for i, p in enumerate(peers):
        for c in range(2):
            cp = output_copy(c, i, senders[i])
            cp.wait_recv()
            cp.wait_send()
            rcopy(HP.at[c, p], HR.at[c, me], hp_s.at[c, i], hp_r.at[c, i], dp=p).wait_send()
            rcopy(HG.at[c, me], HG.at[c, me], hg_s.at[c, i], hg_r.at[c, i], dp=p).wait_send()
        rcopy(mask, M.at[me], a2a_s.at[2, i], a2a_r.at[2, i], dp=p).wait_send()
        for c, (src, dst) in enumerate(((tokens, X), (grads, G))):
            rcopy(src.at[:, cols(p)], dst.at[rows(me)], a2a_s.at[c, i], a2a_r.at[c, i], dp=p).wait_send()
    for q in quarters:
        own_down(q).wait_send()
        relay_mate(q, 1).wait_send()

        @pl.when(y == 1)
        def _():
            own_mate(q).wait_send()
            relay_down(q).wait_send()

    for c in range(2):
        for k, buf in enumerate((S1, S2, S3)):
            rcopy(buf.at[c], RF.at[c], g_s.at[k, c], rf_r.at[c], adapter=up2).wait_send()


def on_device(n, groups, tokens, grad_out, down_panels, up_panels, seg_adapter):
    held, D, rank = down_panels.shape
    segs = seg_adapter.shape[0]
    reach = 2 * segs
    T = tokens.shape[0]
    W = D // n
    B = held * rank
    position = lax.axis_index("adapter")
    down_rows = jnp.transpose(down_panels, (0, 2, 1)).reshape(B, D)
    up_rows = up_panels.reshape(B, D)
    owner = seg_adapter // held
    pick = jnp.mod(owner - position, groups) * held + seg_adapter - owner * held
    mask = (jnp.arange(reach * B, dtype=jnp.int32)[None, :] // rank == pick[:, None]).astype(jnp.float32)
    mask = jnp.pad(mask, ((0, -segs % 8), (0, 0)))

    any_ = pl.BlockSpec(memory_space=pl.ANY)
    vmem = pl.BlockSpec(memory_space=pltpu.VMEM)
    bf, f32 = jnp.bfloat16, jnp.float32
    dma = pltpu.SemaphoreType.DMA
    k = n - 1
    rows = n * T
    result = pl.pallas_call(
        functools.partial(step_kernel, n, groups, segs, rank, reach),
        out_shape=(
            jax.ShapeDtypeStruct((T, D), bf),
            jax.ShapeDtypeStruct((T, D), bf),
            jax.ShapeDtypeStruct((B, W), bf),
            jax.ShapeDtypeStruct((B, W), bf),
        ),
        in_specs=[any_] * 4 + [vmem],
        out_specs=(vmem,) * 4,
        scratch_shapes=[
            pltpu.VMEM((rows, W), bf),
            pltpu.VMEM((rows, W), bf),
            pltpu.VMEM((2, reach, B, W), bf),
            pltpu.VMEM((n,) + mask.shape, f32),
            pltpu.VMEM((2, n, T, B), f32),
            pltpu.VMEM((2, n, T, B), f32),
            pltpu.VMEM((2, n, T, B), bf),
            pltpu.VMEM((rows, reach * B), bf),
            pltpu.VMEM((rows, reach * B), bf),
            pltpu.VMEM((rows, W), bf),
            pltpu.VMEM((rows, W), bf),
            pltpu.VMEM((reach, 2, B, W), f32),
        ]
        + [pltpu.VMEM((2, B, W), bf)] * 7
        + [
            dma((5,)), dma((3, k)), dma((3, k)), dma((4, 4)), dma((4, 4)),
            dma((2, k)), dma((2, k)), dma((2, k)), dma((2, k)), dma((2, k)), dma((2, k)),
            dma((3, 2)), dma((2,)), dma((2,)), dma((2,)), dma((2,)),
        ],
        compiler_params=pltpu.CompilerParams(
            collective_id=0, has_side_effects=True, vmem_limit_bytes=40 * 1024 * 1024
        ),
        cost_estimate=pl.CostEstimate(
            flops=12 * rows * W * reach * B, bytes_accessed=16 * 2 ** 20, transcendentals=0
        ),
    )(tokens, grad_out, down_rows, up_rows, mask)
    out, gtok, gdown, gup = result
    gdown = jnp.transpose(gdown.reshape(held, rank, W), (0, 2, 1))
    return out, gtok, gdown, gup.reshape(held, rank, W)


def solution(mesh):
    placed = (
        P(("dp", "adapter"), None),
        P(("dp", "adapter"), None),
        P("adapter", None, None),
        P("adapter", None, None),
        P(("dp", "adapter")),
    )
    return jax.shard_map(
        functools.partial(on_device, mesh.shape["dp"], mesh.shape["adapter"]),
        mesh=mesh,
        in_specs=placed,
        out_specs=(
            P(("dp", "adapter"), None),
            P(("dp", "adapter"), None),
            P("adapter", "dp", None),
            P("adapter", None, "dp"),
        ),
        check_vma=False,
    )
```

time: 130 us -> 146 us (1.12)
  Pallas kernels: 120 us -> 133 us
  local copies, waits for them, and re-layouts: 7.95 us -> 10.6 us
    pallas_call x1, Pallas kernels: 120 us -> 133 us  [on_device(): pl.pallas_call(functools.partial(step_kernel, n, groups, segs, rank, reac...]
    unnamed x8 -> x12, local copies, waits for them, and re-layouts: 6.84 us -> 10.6 us
where the time goes in v2:
time: 146 us; the launch traced here: 145 us
  Pallas kernels  133 us (91%)
  local copies, waits for them, and re-layouts  10.6 us (7%)
    pallas_call x1, Pallas kernels, on_device(): pl.pallas_call(functools.partial(step_kernel, n, groups, segs, rank, reac...  133 us
    unnamed x12, local copies, waits for them, and re-layouts  10.6 us

profile of v2, /device:TPU:0, one launch (start us, length us, event | category | flops | bytes accessed | tf_op | source)
XLA Modules:
  0.0 145.4 jit_solution(3509218688218543068)
XLA Ops:
  0.6 0.7 fusion.5
  1.3 0.1 broadcast_compare_fusion
  1.4 0.0 copy-start
  1.4 1.6 %copy-done = bf16[128,8192]{1,0:T(8,128)(2,1)S(1)} copy-done((bf16[128,8192]{1,0:T(8,128)(2,1)S(1)}, bf16[128,8192]{1,0:T(8,128)(2,1)}, u32[]{:S(2)}) %copy-start) | copy-done | bytes 2097176
  3.0 0.0 copy-start.1
  3.0 1.6 %copy-done.1 = bf16[128,8192]{1,0:T(8,128)(2,1)S(1)} copy-done((bf16[128,8192]{1,0:T(8,128)(2,1)S(1)}, bf16[128,8192]{1,0:T(8,128)(2,1)}, u32[]{:S(2)}) %copy-start.1) | copy-done | bytes 2097176
  4.6 0.0 copy-start.2
  4.6 1.6 %copy-done.2 = bf16[2,8192,64]{1,2,0:T(8,128)(2,1)S(1)} copy-done((bf16[2,8192,64]{1,2,0:T(8,128)(2,1)S(1)}, bf16[2,8192,64]{1,2,0:T(8,128)(2,1)}, u32[]{:S(2)}) %copy-start.2) | copy-done | bytes 2097176
  6.2 0.0 copy-start.3
  6.2 1.6 %copy-done.3 = bf16[2,64,8192]{2,1,0:T(8,128)(2,1)S(1)} copy-done((bf16[2,64,8192]{2,1,0:T(8,128)(2,1)S(1)}, bf16[2,64,8192]{2,1,0:T(8,128)(2,1)}, u32[]{:S(2)}) %copy-start.3) | copy-done | bytes 2097176
  7.8 133.4 %shard_map.84 = (bf16[128,8192]{1,0:T(8,128)(2,1)S(1)}, bf16[128,8192]{1,0:T(8,128)(2,1)S(1)}, bf16[128,2048]{1,0:T(8,128)(2,1)S(1)}, bf16[128,2048]{1,0:T(8,128)(2,1)S(1)}) custom-call(bf16[128,8192]{1,0:T(8,128)(2,1)S(1)} %copy-done, bf16[128,8192]{1,0:T(8,128)(2,1)S(1)} %copy-done.1, bf16[128,8192]{1,0:T(8,128)(2,1)S(1)} %bitcast.10, ...), custom_call_target="tpu_custom_call" | custom-call | flops 6442450944 | bytes 16777216 | tf_op jit(solution)/shard_map/pallas_call | solution.py:367
  141.2 1.3 copy.13
  142.5 1.3 copy.14
  143.8 0.8 copy.15
  144.6 0.8 copy.16
  (2 shorter events, 0.0 us)
Async XLA Ops:
  1.4 1.6 %copy-start = (bf16[128,8192]{1,0:T(8,128)(2,1)S(1)}, bf16[128,8192]{1,0:T(8,128)(2,1)}, u32[]{:S(2)}) copy-start(bf16[128,8192]{1,0:T(8,128)(2,1)} %tokens.1) | copy-start | bytes 6291460
  3.0 1.6 %copy-start.1 = (bf16[128,8192]{1,0:T(8,128)(2,1)S(1)}, bf16[128,8192]{1,0:T(8,128)(2,1)}, u32[]{:S(2)}) copy-start(bf16[128,8192]{1,0:T(8,128)(2,1)} %grads.1) | copy-start | bytes 6291460
  4.6 1.6 %copy-start.2 = (bf16[2,8192,64]{1,2,0:T(8,128)(2,1)S(1)}, bf16[2,8192,64]{1,2,0:T(8,128)(2,1)}, u32[]{:S(2)}) copy-start(bf16[2,8192,64]{1,2,0:T(8,128)(2,1)} %param.7) | copy-start | bytes 6291460
  6.2 1.6 %copy-start.3 = (bf16[2,64,8192]{2,1,0:T(8,128)(2,1)S(1)}, bf16[2,64,8192]{2,1,0:T(8,128)(2,1)}, u32[]{:S(2)}) copy-start(bf16[2,64,8192]{2,1,0:T(8,128)(2,1)} %param.8) | copy-start | bytes 6291460

commit v3 on v1

--- a/solution.py
+++ b/solution.py
@@ -327,7 +327,7 @@
             jax.ShapeDtypeStruct((B, W), bf),
         ),
         in_specs=[any_, any_, any_, vmem],
-        out_specs=(any_, any_, vmem, vmem),
+        out_specs=(vmem,) * 4,
         scratch_shapes=[
             pltpu.VMEM((rows, W), bf),
             pltpu.VMEM((rows, W), bf),
@@ -349,7 +349,7 @@
             dma((3, 2)), dma((2,)), dma((2,)), dma((2,)), dma((2,)),
         ],
         compiler_params=pltpu.CompilerParams(
-            collective_id=0, has_side_effects=True, vmem_limit_bytes=50 * 1024 * 1024
+            collective_id=0, has_side_effects=True, vmem_limit_bytes=46 * 1024 * 1024
         ),
         cost_estimate=pl.CostEstimate(
             flops=12 * rows * W * reach * B, bytes_accessed=16 * 2 ** 20, transcendentals=0

time: 130 us -> 128 us (0.985)
  local copies, waits for them, and re-layouts: 7.95 us -> 6.03 us
    unnamed x8 -> x6, local copies, waits for them, and re-layouts: 6.84 us -> 4.91 us
where the time goes in v3:
time: 128 us; the launch traced here: 127 us
  Pallas kernels  120 us (94%)
  local copies, waits for them, and re-layouts  6.03 us (5%)
    pallas_call x1, Pallas kernels, on_device(): pl.pallas_call(functools.partial(step_kernel, n, groups, segs, rank, reac...  120 us
    unnamed x6, local copies, waits for them, and re-layouts  4.91 us

profile of v3, /device:TPU:0, one launch (start us, length us, event | category | flops | bytes accessed | tf_op | source)
XLA Modules:
  0.0 127.5 jit_solution(8784130623123786178)
XLA Ops:
  0.6 0.0 copy-start
  0.7 0.8 fusion.5
  1.5 0.1 broadcast_compare_fusion
  1.6 0.7 copy-done
  2.3 1.1 constant_dynamic-slice_fusion
  3.4 0.1 pad_maximum_fusion.pack
  3.5 119.7 %shard_map.84 = (bf16[128,8192]{1,0:T(8,128)(2,1)S(1)}, bf16[128,8192]{1,0:T(8,128)(2,1)S(1)}, bf16[128,2048]{1,0:T(8,128)(2,1)S(1)}, bf16[128,2048]{1,0:T(8,128)(2,1)S(1)}) custom-call(bf16[128,8192]{1,0:T(8,128)(2,1)} %tokens.1, bf16[128,8192]{1,0:T(8,128)(2,1)} %grads.1, bf16[2,128,2048]{2,1,0:T(8,128)(2,1)S(1)} %pad_maximum_fusion.pack, ...), custom_call_target="tpu_custom_call" | custom-call | flops 6442450944 | bytes 16777216 | tf_op jit(solution)/shard_map/pallas_call | solution.py:321
  123.2 1.3 %copy.13 = bf16[128,8192]{1,0:T(8,128)(2,1)} copy(bf16[128,8192]{1,0:T(8,128)(2,1)S(1)} %get-tuple-element.16) | data formatting | bytes 4194304
  124.6 1.3 %copy.14 = bf16[128,8192]{1,0:T(8,128)(2,1)} copy(bf16[128,8192]{1,0:T(8,128)(2,1)S(1)} %get-tuple-element.17) | data formatting | bytes 4194304
  125.9 0.8 copy.15
  126.7 0.8 copy.16
  (3 shorter events, 0.0 us)
Async XLA Ops:
  0.6 1.6 %copy-start = (bf16[2,8192,64]{1,2,0:T(8,128)(2,1)S(1)}, bf16[2,8192,64]{1,2,0:T(8,128)(2,1)}, u32[]{:S(2)}) copy-start(bf16[2,8192,64]{1,2,0:T(8,128)(2,1)} %param.7) | copy-start | bytes 6291460

commit v4 on v3

--- a/solution.py
+++ b/solution.py
@@ -13,7 +13,7 @@
 
 def step_kernel(
     n, groups, segs, rank, reach,
-    tokens, grads, pack, mask, out, gtok, gdown, gup,
+    tokens, grads, down, up, mask, out, gtok, gdown, gup,
     X, G, PP, M, HP, HR, HG, Hm, Gm, OB, TB, C, RA, RB, RC, RF, S1, S2, S3,
     loc, a2a_s, a2a_r, pan_s, pan_r, hp_s, hp_r, hg_s, hg_r, ob_s, ob_r,
     g_s, ra_r, rb_r, rc_r, rf_r,
@@ -46,6 +46,7 @@
             src_ref=src, dst_ref=dst, send_sem=s, recv_sem=r, device_id=dev, device_id_type=MESH
         )
 
+    pack = [down.at[:, cols(me)], up.at[:, cols(me)]]
     barrier = pltpu.get_barrier_semaphore()
     for p in peers:
         pl.semaphore_signal(barrier, inc=1, device_id={"dp": p}, device_id_type=MESH)
@@ -54,12 +55,12 @@
     pl.semaphore_wait(barrier, np_ + 3)
 
     for c in range(2):
-        rcopy(pack.at[c], PP.at[c, 2], pan_s.at[0, c], pan_r.at[2, c], adapter=down2).start()
+        rcopy(pack[c], PP.at[c, 2], pan_s.at[0, c], pan_r.at[2, c], adapter=down2).start()
 
     @pl.when(y == 1)
     def _():
         for c in range(2):
-            rcopy(pack.at[c], PP.at[c, 1], pan_s.at[1, c], pan_r.at[1, c], adapter=mate).start()
+            rcopy(pack[c], PP.at[c, 1], pan_s.at[1, c], pan_r.at[1, c], adapter=mate).start()
 
     for i, p in enumerate(peers):
         rcopy(mask, M.at[me], a2a_s.at[2, i], a2a_r.at[2, i], dp=p).start()
@@ -69,8 +70,8 @@
     locals_ = [
         pltpu.make_async_copy(tokens.at[:, cols(me)], X.at[rows(me)], loc.at[0]),
         pltpu.make_async_copy(grads.at[:, cols(me)], G.at[rows(me)], loc.at[1]),
-        pltpu.make_async_copy(pack.at[0], PP.at[0, 0], loc.at[2]),
-        pltpu.make_async_copy(pack.at[1], PP.at[1, 0], loc.at[3]),
+        pltpu.make_async_copy(pack[0], PP.at[0, 0], loc.at[2]),
+        pltpu.make_async_copy(pack[1], PP.at[1, 0], loc.at[3]),
         pltpu.make_async_copy(mask, M.at[me], loc.at[4]),
     ]
     for cp in locals_:
@@ -79,7 +80,7 @@
         cp.wait()
 
     def pan_wait(slot, c):
-        rcopy(pack.at[c], PP.at[c, slot], pan_s.at[0, c], pan_r.at[slot, c], adapter=down2).wait_recv()
+        rcopy(pack[c], PP.at[c, slot], pan_s.at[0, c], pan_r.at[slot, c], adapter=down2).wait_recv()
 
     for c in range(2):
         pan_wait(2, c)
@@ -167,16 +168,20 @@
     tile = min(W, 512)
     tn = (((0,), (0,)), ((), ()))
 
-    def contribution(k):
+    def half_contribution(k, c):
         ks = slice(k * B, (k + 1) * B)
+        wide, src = ((Gm, X), (Hm, G))[c]
 
         @pl.loop(0, W // tile)
         def _(t):
             at = pl.ds(pl.multiple_of(t * tile, tile), tile)
-            C[k, 0, :, at] = lax.dot_general(Gm[:, ks], X[:, at], tn, preferred_element_type=jnp.float32)
-            C[k, 1, :, at] = scale * lax.dot_general(
-                Hm[:, ks], G[:, at], tn, preferred_element_type=jnp.float32
+            C[k, c, :, at] = (1.0, scale)[c] * lax.dot_general(
+                wide[:, ks], src[:, at], tn, preferred_element_type=jnp.float32
             )
+
+    def contribution(k):
+        half_contribution(k, 0)
+        half_contribution(k, 1)
 
     def outputs(p):
         @pl.loop(0, W // tile)
@@ -199,8 +204,8 @@
         rcopy(OB.at[rows(p)], out.at[:, cols(me)], ob_s.at[0, i], ob_r.at[0, i], dp=p).start()
         rcopy(TB.at[rows(p)], gtok.at[:, cols(me)], ob_s.at[1, i], ob_r.at[1, i], dp=p).start()
 
-    contribution(3)
-    for c in range(2):
+    for c in range(2):
+        half_contribution(3, c)
         S3[c] = C[3, c].astype(jnp.bfloat16)
 
         @pl.when(y == 0)
@@ -283,12 +288,12 @@
         rcopy(HP.at[p], HR.at[me], hp_s.at[i], hp_r.at[i], dp=p).wait_send()
         rcopy(HG.at[me], HG.at[me], hg_s.at[i], hg_r.at[i], dp=p).wait_send()
     for c in range(2):
-        rcopy(pack.at[c], PP.at[c, 2], pan_s.at[0, c], pan_r.at[2, c], adapter=down2).wait_send()
+        rcopy(pack[c], PP.at[c, 2], pan_s.at[0, c], pan_r.at[2, c], adapter=down2).wait_send()
         rcopy(PP.at[c, 2], PP.at[c, 1], pan_s.at[2, c], pan_r.at[1, c], adapter=mate).wait_send()
 
         @pl.when(y == 1)
         def _():
-            rcopy(pack.at[c], PP.at[c, 1], pan_s.at[1, c], pan_r.at[1, c], adapter=mate).wait_send()
+            rcopy(pack[c], PP.at[c, 1], pan_s.at[1, c], pan_r.at[1, c], adapter=mate).wait_send()
             rcopy(PP.at[c, 1], PP.at[c, 3], pan_s.at[3, c], pan_r.at[3, c], adapter=down2).wait_send()
 
         for k, buf in enumerate((S1, S2, S3)):
@@ -302,11 +307,9 @@
     T = tokens.shape[0]
     W = D // n
     B = held * rank
-    me = lax.axis_index("dp")
     position = lax.axis_index("adapter")
-    down_mine = lax.dynamic_slice_in_dim(down_panels, me * W, W, 1)
-    up_mine = lax.dynamic_slice_in_dim(up_panels, me * W, W, 2)
-    pack = jnp.stack([jnp.transpose(down_mine, (0, 2, 1)).reshape(B, W), up_mine.reshape(B, W)])
+    down_rows = jnp.transpose(down_panels, (0, 2, 1)).reshape(B, D)
+    up_rows = up_panels.reshape(B, D)
     owner = seg_adapter // held
     pick = jnp.mod(owner - position, groups) * held + seg_adapter - owner * held
     mask = (jnp.arange(reach * B, dtype=jnp.int32)[None, :] // rank == pick[:, None]).astype(jnp.float32)
@@ -326,7 +329,7 @@
             jax.ShapeDtypeStruct((B, W), bf),
             jax.ShapeDtypeStruct((B, W), bf),
         ),
-        in_specs=[any_, any_, any_, vmem],
+        in_specs=[any_] * 4 + [vmem],
         out_specs=(vmem,) * 4,
         scratch_shapes=[
             pltpu.VMEM((rows, W), bf),
@@ -349,12 +352,12 @@
             dma((3, 2)), dma((2,)), dma((2,)), dma((2,)), dma((2,)),
         ],
         compiler_params=pltpu.CompilerParams(
-            collective_id=0, has_side_effects=True, vmem_limit_bytes=46 * 1024 * 1024
+            collective_id=0, has_side_effects=True, vmem_limit_bytes=48 * 1024 * 1024
         ),
         cost_estimate=pl.CostEstimate(
             flops=12 * rows * W * reach * B, bytes_accessed=16 * 2 ** 20, transcendentals=0
         ),
-    )(tokens, grad_out, pack, mask)
+    )(tokens, grad_out, down_rows, up_rows, mask)
     out, gtok, gdown, gup = result
     gdown = jnp.transpose(gdown.reshape(held, rank, W), (0, 2, 1))
     return out, gtok, gdown, gup.reshape(held, rank, W)

time: 128 us -> 125 us (0.977)
  local copies, waits for them, and re-layouts: 6.03 us -> 4.23 us
    unnamed x6 -> x4, local copies, waits for them, and re-layouts: 4.91 us -> 4.23 us
where the time goes in v4:
time: 125 us
  Pallas kernels  119 us (95%)
  local copies, waits for them, and re-layouts  4.23 us (3%)
    pallas_call x1, Pallas kernels, on_device(): pl.pallas_call(functools.partial(step_kernel, n, groups, segs, rank, reac...  119 us
    unnamed x4, local copies, waits for them, and re-layouts  4.23 us

profile of v4, /device:TPU:0, one launch (start us, length us, event | category | flops | bytes accessed | tf_op | source)
XLA Modules:
  0.0 125.1 jit_solution(6564408570847905672)
XLA Ops:
  0.6 0.7 fusion.5
  1.3 0.1 broadcast_compare_fusion
  1.4 119.4 %shard_map.84 = (bf16[128,8192]{1,0:T(8,128)(2,1)S(1)}, bf16[128,8192]{1,0:T(8,128)(2,1)S(1)}, bf16[128,2048]{1,0:T(8,128)(2,1)S(1)}, bf16[128,2048]{1,0:T(8,128)(2,1)S(1)}) custom-call(bf16[128,8192]{1,0:T(8,128)(2,1)} %tokens.1, bf16[128,8192]{1,0:T(8,128)(2,1)} %grads.1, bf16[128,8192]{1,0:T(8,128)(2,1)} %bitcast.10, bf16[128,8192]{1,0:T(8,128)(2,1)} %bitcast.11, ...), custom_call_target="tpu_custom_call" | custom-call | flops 6442450944 | bytes 16777216 | tf_op jit(solution)/shard_map/pallas_call | solution.py:324
  120.8 1.3 %copy.13 = bf16[128,8192]{1,0:T(8,128)(2,1)} copy(bf16[128,8192]{1,0:T(8,128)(2,1)S(1)} %get-tuple-element.16) | data formatting | bytes 4194304
  122.2 1.3 %copy.14 = bf16[128,8192]{1,0:T(8,128)(2,1)} copy(bf16[128,8192]{1,0:T(8,128)(2,1)S(1)} %get-tuple-element.17) | data formatting | bytes 4194304
  123.5 0.8 copy.15
  124.3 0.8 copy.16
  (2 shorter events, 0.0 us)
